TPU v7x, 512 devices: a whole 4x4x16 slice. The times are simulated.
512 devices in a mesh: seq: 64 (over x, z), head: 8 (over y, core).
Axes of the slice: x: 4, y: 4, z: 16, core: 2. Of those that a mesh axis runs over, the one named last changes fastest.
Arguments:
- queries: bfloat16 [32768, 1024], P('seq', 'head'), may hold values from -13 to 13
- keys: bfloat16 [32768, 128], P(('seq', 'head')), may hold values from -4.5 to 4.5
- values: bfloat16 [32768, 128], P(('seq', 'head')), may hold values from -6 to 6
- req_lengths: int32 [16], replicated, may hold values from 1 to 128, 256 in all
Outputs:
- attended: bfloat16 [32768, 1024], P('seq', 'head')
Inputs may be any that keep to these rules, and one draw needn't show every extreme that they name: `req_lengths`: requests cover all 32768 tokens end to end; the longest has exactly 16384 tokens.
All inputs are finite; a program needn't handle non-finite values.
Results may differ from a plain program's by a relative error of at most 0.0045.
Values may be sent and summed in bfloat16 or wider, within the bound.
A program may use at most 64 MiB of HBM per device.

v0:
```python
import math

import jax
import jax.numpy as jnp
from jax import lax
from jax.sharding import PartitionSpec as P

HD = 128
PAGE = 128


NEG_FILL = -1e30


def passed_along(value, axis, by):
    length = lax.axis_size(axis)
    pairs = [(i, i + by) for i in range(length) if 0 <= i + by < length]
    return lax.ppermute(value, axis, pairs)


def token_starts(req_lengths, first_token, row_count):
    lengths = req_lengths * PAGE
    request_ends = jnp.cumsum(lengths)
    request_starts = request_ends - lengths
    positions = first_token + jnp.arange(row_count, dtype=jnp.int32)
    inside = request_starts[None, :] <= positions[:, None]
    return jnp.max(jnp.where(inside, request_starts[None, :], 0), axis=1)


def attend_dense(running, kv_pair, distance, context, row_offset):
    query_heads, query_pos, query_start, seq_position, tok_rows = context
    summed, row_max, totals = running
    key_count = kv_pair[0].shape[0]
    key_pos = (
        (seq_position - distance) * tok_rows + row_offset + jnp.arange(key_count, dtype=jnp.int32)
    )
    visible = (key_pos[None, :] >= query_start[:, None]) & (key_pos[None, :] <= query_pos[:, None])
    scores = jnp.einsum("qhd,kd->hqk", query_heads, kv_pair[0], preferred_element_type=jnp.float32)
    scores = scores * (1.0 / math.sqrt(HD))
    block_max = jnp.max(jnp.where(visible[None], scores, NEG_FILL), axis=2)
    new_max = jnp.maximum(row_max, block_max)
    exp_terms = jnp.where(visible[None], jnp.exp(scores - new_max[:, :, None]), 0.0)
    factor = jnp.exp(row_max - new_max)
    totals = totals * factor + jnp.sum(exp_terms, axis=2)
    weights = exp_terms.astype(jnp.bfloat16)
    update = jnp.einsum("hqk,kd->hqd", weights, kv_pair[1], preferred_element_type=jnp.float32)
    summed = summed * factor[:, :, None] + update
    return (summed, new_max, totals)


def attend(running, kv_pair, distance, context, row_offset=0):
    return attend_dense(running, kv_pair, distance, context, row_offset)


def body(queries, keys, values, req_lengths):
    tok_rows = queries.shape[0]
    heads_here = queries.shape[1] // HD
    span_blocks = lax.axis_size("seq") // 2
    seq_position = lax.axis_index("seq")
    first_token = seq_position * tok_rows
    query_pos = first_token + jnp.arange(tok_rows, dtype=jnp.int32)
    query_start = token_starts(req_lengths, first_token, tok_rows)
    query_heads = queries.reshape(tok_rows, heads_here, HD)
    context = (query_heads, query_pos, query_start, seq_position, tok_rows)
    own_slice = jnp.stack((keys, values))
    own_pair = lax.all_gather(own_slice, "head", axis=1, tiled=True)
    running = (
        jnp.zeros((heads_here, tok_rows, HD), jnp.float32),
        jnp.full((heads_here, tok_rows), NEG_FILL, jnp.float32),
        jnp.zeros((heads_here, tok_rows), jnp.float32),
    )
    running = attend(running, own_pair, 0, context)

    def relay_turn(turn_index, carried):
        moving, partial_value = carried
        moving = passed_along(moving, "seq", 1)
        return (moving, attend(partial_value, moving, turn_index, context))

    moving, running = lax.fori_loop(1, span_blocks + 1, relay_turn, (own_pair, running))
    summed, row_max, totals = running
    output = summed / totals[:, :, None]
    return jnp.transpose(output, (1, 0, 2)).reshape(tok_rows, heads_here * HD).astype(jnp.bfloat16)


def solution(mesh):
    placed = (P("seq", "head"), P(("seq", "head"), None), P(("seq", "head"), None), P())
    return jax.shard_map(
        body, mesh=mesh, in_specs=placed, out_specs=P("seq", "head"), check_vma=False
    )
```

profile of v0, /device:TPU:6, one launch (start us, length us, event | category | flops | bytes accessed | tf_op | source)
XLA Modules:
  0.0 418.5 jit_solution(10336718525045193828)
XLA Ops:
  1.5 13.5 %all_gather.3 = bf16[2,512,128]{2,1,0:T(8,128)(2,1)S(1)} all-gather(bf16[2,64,128]{2,1,0:T(8,128)(2,1)S(1)} %pad_maximum_fusion), channel_id=1, replica_groups=mesh['seq'=64,'head'=8] {'head'}, dimensions={1}, use_global_device_ids=true | all-gather | bytes 294912 | tf_op jit(solution)/shard_map/all_gather | solution.py:66
  16.2 401.5 %while.20 = (s32[]{:T(128)}, bf16[2,512,128]{2,1,0:T(8,128)(2,1)S(1)}, f32[1,512,128]{2,1,0:T(8,128)S(1)}, f32[1,512]{1,0:T(1,128)S(1)}, f32[1,512]{1,0:T(1,128)...) while((s32[]{:T(128)}, ...), condition=%wide.region_7.8_spmd.clone, body=%wide.region_4.7_spmd.clone.sunk | while | flops 139069440 | bytes 5691573 | solution.py:79
  20.1 14.6 %collective-permute-done = bf16[2,512,128]{2,1,0:T(8,128)(2,1)S(1)} collective-permute-done((bf16[2,512,128]{2,1,0:T(8,128)(2,1)S(1)}, bf16[2,512,128]{2,1,0:T(8,128)(2,1)S(1)}, u32[]{:S(2)}, u32[]{:S(2)}) %collective-permute-start) | collective-permute-done | bytes 262176 | tf_op jit(solution)/shard_map/while/body/eval_jaxpr/ppermute | solution.py:18
  38.0 10.1 %collective-permute-done = bf16[2,512,128]{2,1,0:T(8,128)(2,1)S(1)} collective-permute-done((bf16[2,512,128]{2,1,0:T(8,128)(2,1)S(1)}, bf16[2,512,128]{2,1,0:T(8,128)(2,1)S(1)}, u32[]{:S(2)}, u32[]{:S(2)}) %collective-permute-start) | collective-permute-done | bytes 262176 | tf_op jit(solution)/shard_map/while/body/eval_jaxpr/ppermute | solution.py:18
  51.4 9.3 %collective-permute-done = bf16[2,512,128]{2,1,0:T(8,128)(2,1)S(1)} collective-permute-done((bf16[2,512,128]{2,1,0:T(8,128)(2,1)S(1)}, bf16[2,512,128]{2,1,0:T(8,128)(2,1)S(1)}, u32[]{:S(2)}, u32[]{:S(2)}) %collective-permute-start) | collective-permute-done | bytes 262176 | tf_op jit(solution)/shard_map/while/body/eval_jaxpr/ppermute | solution.py:18
  63.9 8.4 %collective-permute-done = bf16[2,512,128]{2,1,0:T(8,128)(2,1)S(1)} collective-permute-done((bf16[2,512,128]{2,1,0:T(8,128)(2,1)S(1)}, bf16[2,512,128]{2,1,0:T(8,128)(2,1)S(1)}, u32[]{:S(2)}, u32[]{:S(2)}) %collective-permute-start) | collective-permute-done | bytes 262176 | tf_op jit(solution)/shard_map/while/body/eval_jaxpr/ppermute | solution.py:18
  75.6 8.4 %collective-permute-done = bf16[2,512,128]{2,1,0:T(8,128)(2,1)S(1)} collective-permute-done((bf16[2,512,128]{2,1,0:T(8,128)(2,1)S(1)}, bf16[2,512,128]{2,1,0:T(8,128)(2,1)S(1)}, u32[]{:S(2)}, u32[]{:S(2)}) %collective-permute-start) | collective-permute-done | bytes 262176 | tf_op jit(solution)/shard_map/while/body/eval_jaxpr/ppermute | solution.py:18
  87.3 8.4 %collective-permute-done = bf16[2,512,128]{2,1,0:T(8,128)(2,1)S(1)} collective-permute-done((bf16[2,512,128]{2,1,0:T(8,128)(2,1)S(1)}, bf16[2,512,128]{2,1,0:T(8,128)(2,1)S(1)}, u32[]{:S(2)}, u32[]{:S(2)}) %collective-permute-start) | collective-permute-done | bytes 262176 | tf_op jit(solution)/shard_map/while/body/eval_jaxpr/ppermute | solution.py:18
  99.0 8.4 %collective-permute-done = bf16[2,512,128]{2,1,0:T(8,128)(2,1)S(1)} collective-permute-done((bf16[2,512,128]{2,1,0:T(8,128)(2,1)S(1)}, bf16[2,512,128]{2,1,0:T(8,128)(2,1)S(1)}, u32[]{:S(2)}, u32[]{:S(2)}) %collective-permute-start) | collective-permute-done | bytes 262176 | tf_op jit(solution)/shard_map/while/body/eval_jaxpr/ppermute | solution.py:18
  110.7 8.4 %collective-permute-done = bf16[2,512,128]{2,1,0:T(8,128)(2,1)S(1)} collective-permute-done((bf16[2,512,128]{2,1,0:T(8,128)(2,1)S(1)}, bf16[2,512,128]{2,1,0:T(8,128)(2,1)S(1)}, u32[]{:S(2)}, u32[]{:S(2)}) %collective-permute-start) | collective-permute-done | bytes 262176 | tf_op jit(solution)/shard_map/while/body/eval_jaxpr/ppermute | solution.py:18
  122.4 9.3 %collective-permute-done = bf16[2,512,128]{2,1,0:T(8,128)(2,1)S(1)} collective-permute-done((bf16[2,512,128]{2,1,0:T(8,128)(2,1)S(1)}, bf16[2,512,128]{2,1,0:T(8,128)(2,1)S(1)}, u32[]{:S(2)}, u32[]{:S(2)}) %collective-permute-start) | collective-permute-done | bytes 262176 | tf_op jit(solution)/shard_map/while/body/eval_jaxpr/ppermute | solution.py:18
  135.0 10.4 %collective-permute-done = bf16[2,512,128]{2,1,0:T(8,128)(2,1)S(1)} collective-permute-done((bf16[2,512,128]{2,1,0:T(8,128)(2,1)S(1)}, bf16[2,512,128]{2,1,0:T(8,128)(2,1)S(1)}, u32[]{:S(2)}, u32[]{:S(2)}) %collective-permute-start) | collective-permute-done | bytes 262176 | tf_op jit(solution)/shard_map/while/body/eval_jaxpr/ppermute | solution.py:18
  148.7 10.9 %collective-permute-done = bf16[2,512,128]{2,1,0:T(8,128)(2,1)S(1)} collective-permute-done((bf16[2,512,128]{2,1,0:T(8,128)(2,1)S(1)}, bf16[2,512,128]{2,1,0:T(8,128)(2,1)S(1)}, u32[]{:S(2)}, u32[]{:S(2)}) %collective-permute-start) | collective-permute-done | bytes 262176 | tf_op jit(solution)/shard_map/while/body/eval_jaxpr/ppermute | solution.py:18
  162.8 10.0 %collective-permute-done = bf16[2,512,128]{2,1,0:T(8,128)(2,1)S(1)} collective-permute-done((bf16[2,512,128]{2,1,0:T(8,128)(2,1)S(1)}, bf16[2,512,128]{2,1,0:T(8,128)(2,1)S(1)}, u32[]{:S(2)}, u32[]{:S(2)}) %collective-permute-start) | collective-permute-done | bytes 262176 | tf_op jit(solution)/shard_map/while/body/eval_jaxpr/ppermute | solution.py:18
  176.2 9.2 %collective-permute-done = bf16[2,512,128]{2,1,0:T(8,128)(2,1)S(1)} collective-permute-done((bf16[2,512,128]{2,1,0:T(8,128)(2,1)S(1)}, bf16[2,512,128]{2,1,0:T(8,128)(2,1)S(1)}, u32[]{:S(2)}, u32[]{:S(2)}) %collective-permute-start) | collective-permute-done | bytes 262176 | tf_op jit(solution)/shard_map/while/body/eval_jaxpr/ppermute | solution.py:18
  188.6 8.4 %collective-permute-done = bf16[2,512,128]{2,1,0:T(8,128)(2,1)S(1)} collective-permute-done((bf16[2,512,128]{2,1,0:T(8,128)(2,1)S(1)}, bf16[2,512,128]{2,1,0:T(8,128)(2,1)S(1)}, u32[]{:S(2)}, u32[]{:S(2)}) %collective-permute-start) | collective-permute-done | bytes 262176 | tf_op jit(solution)/shard_map/while/body/eval_jaxpr/ppermute | solution.py:18
  200.3 8.4 %collective-permute-done = bf16[2,512,128]{2,1,0:T(8,128)(2,1)S(1)} collective-permute-done((bf16[2,512,128]{2,1,0:T(8,128)(2,1)S(1)}, bf16[2,512,128]{2,1,0:T(8,128)(2,1)S(1)}, u32[]{:S(2)}, u32[]{:S(2)}) %collective-permute-start) | collective-permute-done | bytes 262176 | tf_op jit(solution)/shard_map/while/body/eval_jaxpr/ppermute | solution.py:18
  212.0 8.4 %collective-permute-done = bf16[2,512,128]{2,1,0:T(8,128)(2,1)S(1)} collective-permute-done((bf16[2,512,128]{2,1,0:T(8,128)(2,1)S(1)}, bf16[2,512,128]{2,1,0:T(8,128)(2,1)S(1)}, u32[]{:S(2)}, u32[]{:S(2)}) %collective-permute-start) | collective-permute-done | bytes 262176 | tf_op jit(solution)/shard_map/while/body/eval_jaxpr/ppermute | solution.py:18
  247.1 9.4 %collective-permute-done = bf16[2,512,128]{2,1,0:T(8,128)(2,1)S(1)} collective-permute-done((bf16[2,512,128]{2,1,0:T(8,128)(2,1)S(1)}, bf16[2,512,128]{2,1,0:T(8,128)(2,1)S(1)}, u32[]{:S(2)}, u32[]{:S(2)}) %collective-permute-start) | collective-permute-done | bytes 262176 | tf_op jit(solution)/shard_map/while/body/eval_jaxpr/ppermute | solution.py:18
  259.8 10.6 %collective-permute-done = bf16[2,512,128]{2,1,0:T(8,128)(2,1)S(1)} collective-permute-done((bf16[2,512,128]{2,1,0:T(8,128)(2,1)S(1)}, bf16[2,512,128]{2,1,0:T(8,128)(2,1)S(1)}, u32[]{:S(2)}, u32[]{:S(2)}) %collective-permute-start) | collective-permute-done | bytes 262176 | tf_op jit(solution)/shard_map/while/body/eval_jaxpr/ppermute | solution.py:18
  273.6 10.8 %collective-permute-done = bf16[2,512,128]{2,1,0:T(8,128)(2,1)S(1)} collective-permute-done((bf16[2,512,128]{2,1,0:T(8,128)(2,1)S(1)}, bf16[2,512,128]{2,1,0:T(8,128)(2,1)S(1)}, u32[]{:S(2)}, u32[]{:S(2)}) %collective-permute-start) | collective-permute-done | bytes 262176 | tf_op jit(solution)/shard_map/while/body/eval_jaxpr/ppermute | solution.py:18
  287.6 10.0 %collective-permute-done = bf16[2,512,128]{2,1,0:T(8,128)(2,1)S(1)} collective-permute-done((bf16[2,512,128]{2,1,0:T(8,128)(2,1)S(1)}, bf16[2,512,128]{2,1,0:T(8,128)(2,1)S(1)}, u32[]{:S(2)}, u32[]{:S(2)}) %collective-permute-start) | collective-permute-done | bytes 262176 | tf_op jit(solution)/shard_map/while/body/eval_jaxpr/ppermute | solution.py:18
  300.9 9.1 %collective-permute-done = bf16[2,512,128]{2,1,0:T(8,128)(2,1)S(1)} collective-permute-done((bf16[2,512,128]{2,1,0:T(8,128)(2,1)S(1)}, bf16[2,512,128]{2,1,0:T(8,128)(2,1)S(1)}, u32[]{:S(2)}, u32[]{:S(2)}) %collective-permute-start) | collective-permute-done | bytes 262176 | tf_op jit(solution)/shard_map/while/body/eval_jaxpr/ppermute | solution.py:18
  371.8 9.4 %collective-permute-done = bf16[2,512,128]{2,1,0:T(8,128)(2,1)S(1)} collective-permute-done((bf16[2,512,128]{2,1,0:T(8,128)(2,1)S(1)}, bf16[2,512,128]{2,1,0:T(8,128)(2,1)S(1)}, u32[]{:S(2)}, u32[]{:S(2)}) %collective-permute-start) | collective-permute-done | bytes 262176 | tf_op jit(solution)/shard_map/while/body/eval_jaxpr/ppermute | solution.py:18
  (320 shorter events, 192.4 us)
Async XLA Ops:
  16.2 18.5 %collective-permute-start = (bf16[2,512,128]{2,1,0:T(8,128)(2,1)S(1)}, bf16[2,512,128]{2,1,0:T(8,128)(2,1)S(1)}, u32[]{:S(2)}, u32[]{:S(2)}) collective-permute-start(bf16[2,512,128]{2,1,0:T(8,128)(2,1)S(1)} %get-tuple-element.290), channel_id=1, source_target_pairs={{0,8},{8,16},{16,24},{24,32},{32,40},{40,48},{48,56},{56,64},{64,7... | collective-permute-start | bytes 786440 | tf_op jit(solution)/shard_map/while/body/eval_jaxpr/ppermute | solution.py:18
  36.0 12.1 %collective-permute-start = (bf16[2,512,128]{2,1,0:T(8,128)(2,1)S(1)}, bf16[2,512,128]{2,1,0:T(8,128)(2,1)S(1)}, u32[]{:S(2)}, u32[]{:S(2)}) collective-permute-start(bf16[2,512,128]{2,1,0:T(8,128)(2,1)S(1)} %get-tuple-element.290), channel_id=1, source_target_pairs={{0,8},{8,16},{16,24},{24,32},{32,40},{40,48},{48,56},{56,64},{64,7... | collective-permute-start | bytes 786440 | tf_op jit(solution)/shard_map/while/body/eval_jaxpr/ppermute | solution.py:18
  49.4 11.2 %collective-permute-start = (bf16[2,512,128]{2,1,0:T(8,128)(2,1)S(1)}, bf16[2,512,128]{2,1,0:T(8,128)(2,1)S(1)}, u32[]{:S(2)}, u32[]{:S(2)}) collective-permute-start(bf16[2,512,128]{2,1,0:T(8,128)(2,1)S(1)} %get-tuple-element.290), channel_id=1, source_target_pairs={{0,8},{8,16},{16,24},{24,32},{32,40},{40,48},{48,56},{56,64},{64,7... | collective-permute-start | bytes 786440 | tf_op jit(solution)/shard_map/while/body/eval_jaxpr/ppermute | solution.py:18
  62.0 10.4 %collective-permute-start = (bf16[2,512,128]{2,1,0:T(8,128)(2,1)S(1)}, bf16[2,512,128]{2,1,0:T(8,128)(2,1)S(1)}, u32[]{:S(2)}, u32[]{:S(2)}) collective-permute-start(bf16[2,512,128]{2,1,0:T(8,128)(2,1)S(1)} %get-tuple-element.290), channel_id=1, source_target_pairs={{0,8},{8,16},{16,24},{24,32},{32,40},{40,48},{48,56},{56,64},{64,7... | collective-permute-start | bytes 786440 | tf_op jit(solution)/shard_map/while/body/eval_jaxpr/ppermute | solution.py:18
  73.7 10.4 %collective-permute-start = (bf16[2,512,128]{2,1,0:T(8,128)(2,1)S(1)}, bf16[2,512,128]{2,1,0:T(8,128)(2,1)S(1)}, u32[]{:S(2)}, u32[]{:S(2)}) collective-permute-start(bf16[2,512,128]{2,1,0:T(8,128)(2,1)S(1)} %get-tuple-element.290), channel_id=1, source_target_pairs={{0,8},{8,16},{16,24},{24,32},{32,40},{40,48},{48,56},{56,64},{64,7... | collective-permute-start | bytes 786440 | tf_op jit(solution)/shard_map/while/body/eval_jaxpr/ppermute | solution.py:18
  85.4 10.4 %collective-permute-start = (bf16[2,512,128]{2,1,0:T(8,128)(2,1)S(1)}, bf16[2,512,128]{2,1,0:T(8,128)(2,1)S(1)}, u32[]{:S(2)}, u32[]{:S(2)}) collective-permute-start(bf16[2,512,128]{2,1,0:T(8,128)(2,1)S(1)} %get-tuple-element.290), channel_id=1, source_target_pairs={{0,8},{8,16},{16,24},{24,32},{32,40},{40,48},{48,56},{56,64},{64,7... | collective-permute-start | bytes 786440 | tf_op jit(solution)/shard_map/while/body/eval_jaxpr/ppermute | solution.py:18
  97.1 10.4 %collective-permute-start = (bf16[2,512,128]{2,1,0:T(8,128)(2,1)S(1)}, bf16[2,512,128]{2,1,0:T(8,128)(2,1)S(1)}, u32[]{:S(2)}, u32[]{:S(2)}) collective-permute-start(bf16[2,512,128]{2,1,0:T(8,128)(2,1)S(1)} %get-tuple-element.290), channel_id=1, source_target_pairs={{0,8},{8,16},{16,24},{24,32},{32,40},{40,48},{48,56},{56,64},{64,7... | collective-permute-start | bytes 786440 | tf_op jit(solution)/shard_map/while/body/eval_jaxpr/ppermute | solution.py:18
  108.8 10.4 %collective-permute-start = (bf16[2,512,128]{2,1,0:T(8,128)(2,1)S(1)}, bf16[2,512,128]{2,1,0:T(8,128)(2,1)S(1)}, u32[]{:S(2)}, u32[]{:S(2)}) collective-permute-start(bf16[2,512,128]{2,1,0:T(8,128)(2,1)S(1)} %get-tuple-element.290), channel_id=1, source_target_pairs={{0,8},{8,16},{16,24},{24,32},{32,40},{40,48},{48,56},{56,64},{64,7... | collective-permute-start | bytes 786440 | tf_op jit(solution)/shard_map/while/body/eval_jaxpr/ppermute | solution.py:18
  120.5 11.2 %collective-permute-start = (bf16[2,512,128]{2,1,0:T(8,128)(2,1)S(1)}, bf16[2,512,128]{2,1,0:T(8,128)(2,1)S(1)}, u32[]{:S(2)}, u32[]{:S(2)}) collective-permute-start(bf16[2,512,128]{2,1,0:T(8,128)(2,1)S(1)} %get-tuple-element.290), channel_id=1, source_target_pairs={{0,8},{8,16},{16,24},{24,32},{32,40},{40,48},{48,56},{56,64},{64,7... | collective-permute-start | bytes 786440 | tf_op jit(solution)/shard_map/while/body/eval_jaxpr/ppermute | solution.py:18
  133.0 12.4 %collective-permute-start = (bf16[2,512,128]{2,1,0:T(8,128)(2,1)S(1)}, bf16[2,512,128]{2,1,0:T(8,128)(2,1)S(1)}, u32[]{:S(2)}, u32[]{:S(2)}) collective-permute-start(bf16[2,512,128]{2,1,0:T(8,128)(2,1)S(1)} %get-tuple-element.290), channel_id=1, source_target_pairs={{0,8},{8,16},{16,24},{24,32},{32,40},{40,48},{48,56},{56,64},{64,7... | collective-permute-start | bytes 786440 | tf_op jit(solution)/shard_map/while/body/eval_jaxpr/ppermute | solution.py:18
  146.7 12.8 %collective-permute-start = (bf16[2,512,128]{2,1,0:T(8,128)(2,1)S(1)}, bf16[2,512,128]{2,1,0:T(8,128)(2,1)S(1)}, u32[]{:S(2)}, u32[]{:S(2)}) collective-permute-start(bf16[2,512,128]{2,1,0:T(8,128)(2,1)S(1)} %get-tuple-element.290), channel_id=1, source_target_pairs={{0,8},{8,16},{16,24},{24,32},{32,40},{40,48},{48,56},{56,64},{64,7... | collective-permute-start | bytes 786440 | tf_op jit(solution)/shard_map/while/body/eval_jaxpr/ppermute | solution.py:18
  160.9 12.0 %collective-permute-start = (bf16[2,512,128]{2,1,0:T(8,128)(2,1)S(1)}, bf16[2,512,128]{2,1,0:T(8,128)(2,1)S(1)}, u32[]{:S(2)}, u32[]{:S(2)}) collective-permute-start(bf16[2,512,128]{2,1,0:T(8,128)(2,1)S(1)} %get-tuple-element.290), channel_id=1, source_target_pairs={{0,8},{8,16},{16,24},{24,32},{32,40},{40,48},{48,56},{56,64},{64,7... | collective-permute-start | bytes 786440 | tf_op jit(solution)/shard_map/while/body/eval_jaxpr/ppermute | solution.py:18
  174.2 11.1 %collective-permute-start = (bf16[2,512,128]{2,1,0:T(8,128)(2,1)S(1)}, bf16[2,512,128]{2,1,0:T(8,128)(2,1)S(1)}, u32[]{:S(2)}, u32[]{:S(2)}) collective-permute-start(bf16[2,512,128]{2,1,0:T(8,128)(2,1)S(1)} %get-tuple-element.290), channel_id=1, source_target_pairs={{0,8},{8,16},{16,24},{24,32},{32,40},{40,48},{48,56},{56,64},{64,7... | collective-permute-start | bytes 786440 | tf_op jit(solution)/shard_map/while/body/eval_jaxpr/ppermute | solution.py:18
  186.6 10.4 %collective-permute-start = (bf16[2,512,128]{2,1,0:T(8,128)(2,1)S(1)}, bf16[2,512,128]{2,1,0:T(8,128)(2,1)S(1)}, u32[]{:S(2)}, u32[]{:S(2)}) collective-permute-start(bf16[2,512,128]{2,1,0:T(8,128)(2,1)S(1)} %get-tuple-element.290), channel_id=1, source_target_pairs={{0,8},{8,16},{16,24},{24,32},{32,40},{40,48},{48,56},{56,64},{64,7... | collective-permute-start | bytes 786440 | tf_op jit(solution)/shard_map/while/body/eval_jaxpr/ppermute | solution.py:18
  198.4 10.4 %collective-permute-start = (bf16[2,512,128]{2,1,0:T(8,128)(2,1)S(1)}, bf16[2,512,128]{2,1,0:T(8,128)(2,1)S(1)}, u32[]{:S(2)}, u32[]{:S(2)}) collective-permute-start(bf16[2,512,128]{2,1,0:T(8,128)(2,1)S(1)} %get-tuple-element.290), channel_id=1, source_target_pairs={{0,8},{8,16},{16,24},{24,32},{32,40},{40,48},{48,56},{56,64},{64,7... | collective-permute-start | bytes 786440 | tf_op jit(solution)/shard_map/while/body/eval_jaxpr/ppermute | solution.py:18
  210.1 10.4 %collective-permute-start = (bf16[2,512,128]{2,1,0:T(8,128)(2,1)S(1)}, bf16[2,512,128]{2,1,0:T(8,128)(2,1)S(1)}, u32[]{:S(2)}, u32[]{:S(2)}) collective-permute-start(bf16[2,512,128]{2,1,0:T(8,128)(2,1)S(1)} %get-tuple-element.290), channel_id=1, source_target_pairs={{0,8},{8,16},{16,24},{24,32},{32,40},{40,48},{48,56},{56,64},{64,7... | collective-permute-start | bytes 786440 | tf_op jit(solution)/shard_map/while/body/eval_jaxpr/ppermute | solution.py:18
  245.2 11.3 %collective-permute-start = (bf16[2,512,128]{2,1,0:T(8,128)(2,1)S(1)}, bf16[2,512,128]{2,1,0:T(8,128)(2,1)S(1)}, u32[]{:S(2)}, u32[]{:S(2)}) collective-permute-start(bf16[2,512,128]{2,1,0:T(8,128)(2,1)S(1)} %get-tuple-element.290), channel_id=1, source_target_pairs={{0,8},{8,16},{16,24},{24,32},{32,40},{40,48},{48,56},{56,64},{64,7... | collective-permute-start | bytes 786440 | tf_op jit(solution)/shard_map/while/body/eval_jaxpr/ppermute | solution.py:18
  257.8 12.5 %collective-permute-start = (bf16[2,512,128]{2,1,0:T(8,128)(2,1)S(1)}, bf16[2,512,128]{2,1,0:T(8,128)(2,1)S(1)}, u32[]{:S(2)}, u32[]{:S(2)}) collective-permute-start(bf16[2,512,128]{2,1,0:T(8,128)(2,1)S(1)} %get-tuple-element.290), channel_id=1, source_target_pairs={{0,8},{8,16},{16,24},{24,32},{32,40},{40,48},{48,56},{56,64},{64,7... | collective-permute-start | bytes 786440 | tf_op jit(solution)/shard_map/while/body/eval_jaxpr/ppermute | solution.py:18
  271.7 12.7 %collective-permute-start = (bf16[2,512,128]{2,1,0:T(8,128)(2,1)S(1)}, bf16[2,512,128]{2,1,0:T(8,128)(2,1)S(1)}, u32[]{:S(2)}, u32[]{:S(2)}) collective-permute-start(bf16[2,512,128]{2,1,0:T(8,128)(2,1)S(1)} %get-tuple-element.290), channel_id=1, source_target_pairs={{0,8},{8,16},{16,24},{24,32},{32,40},{40,48},{48,56},{56,64},{64,7... | collective-permute-start | bytes 786440 | tf_op jit(solution)/shard_map/while/body/eval_jaxpr/ppermute | solution.py:18
  285.7 11.9 %collective-permute-start = (bf16[2,512,128]{2,1,0:T(8,128)(2,1)S(1)}, bf16[2,512,128]{2,1,0:T(8,128)(2,1)S(1)}, u32[]{:S(2)}, u32[]{:S(2)}) collective-permute-start(bf16[2,512,128]{2,1,0:T(8,128)(2,1)S(1)} %get-tuple-element.290), channel_id=1, source_target_pairs={{0,8},{8,16},{16,24},{24,32},{32,40},{40,48},{48,56},{56,64},{64,7... | collective-permute-start | bytes 786440 | tf_op jit(solution)/shard_map/while/body/eval_jaxpr/ppermute | solution.py:18
  299.0 11.0 %collective-permute-start = (bf16[2,512,128]{2,1,0:T(8,128)(2,1)S(1)}, bf16[2,512,128]{2,1,0:T(8,128)(2,1)S(1)}, u32[]{:S(2)}, u32[]{:S(2)}) collective-permute-start(bf16[2,512,128]{2,1,0:T(8,128)(2,1)S(1)} %get-tuple-element.290), channel_id=1, source_target_pairs={{0,8},{8,16},{16,24},{24,32},{32,40},{40,48},{48,56},{56,64},{64,7... | collective-permute-start | bytes 786440 | tf_op jit(solution)/shard_map/while/body/eval_jaxpr/ppermute | solution.py:18
  346.5 10.4 %collective-permute-start = (bf16[2,512,128]{2,1,0:T(8,128)(2,1)S(1)}, bf16[2,512,128]{2,1,0:T(8,128)(2,1)S(1)}, u32[]{:S(2)}, u32[]{:S(2)}) collective-permute-start(bf16[2,512,128]{2,1,0:T(8,128)(2,1)S(1)} %get-tuple-element.290), channel_id=1, source_target_pairs={{0,8},{8,16},{16,24},{24,32},{32,40},{40,48},{48,56},{56,64},{64,7... | collective-permute-start | bytes 786440 | tf_op jit(solution)/shard_map/while/body/eval_jaxpr/ppermute | solution.py:18
  369.9 11.4 %collective-permute-start = (bf16[2,512,128]{2,1,0:T(8,128)(2,1)S(1)}, bf16[2,512,128]{2,1,0:T(8,128)(2,1)S(1)}, u32[]{:S(2)}, u32[]{:S(2)}) collective-permute-start(bf16[2,512,128]{2,1,0:T(8,128)(2,1)S(1)} %get-tuple-element.290), channel_id=1, source_target_pairs={{0,8},{8,16},{16,24},{24,32},{32,40},{40,48},{48,56},{56,64},{64,7... | collective-permute-start | bytes 786440 | tf_op jit(solution)/shard_map/while/body/eval_jaxpr/ppermute | solution.py:18
  406.0 10.4 %collective-permute-start = (bf16[2,512,128]{2,1,0:T(8,128)(2,1)S(1)}, bf16[2,512,128]{2,1,0:T(8,128)(2,1)S(1)}, u32[]{:S(2)}, u32[]{:S(2)}) collective-permute-start(bf16[2,512,128]{2,1,0:T(8,128)(2,1)S(1)} %get-tuple-element.290), channel_id=1, source_target_pairs={{0,8},{8,16},{16,24},{24,32},{32,40},{40,48},{48,56},{56,64},{64,7... | collective-permute-start | bytes 786440 | tf_op jit(solution)/shard_map/while/body/eval_jaxpr/ppermute | solution.py:18
  (12 other events, 98.6 us)
where the time goes:
time: 420 us; the launch traced here: 418 us
  waiting for transfers between devices  295 us (70%)
  starting transfers between devices  63.4 us (15%)
  matrix products  30.4 us (7%)
  blocking collectives  13.5 us (3%)
  other arithmetic  12.5 us (3%)
    ppermute x32, waiting for transfers between devices, passed_along(): return lax.ppermute(value, axis, pairs)  295 us
    ppermute x32, starting transfers between devices, passed_along(): return lax.ppermute(value, axis, pairs)  63.4 us
    dot_general x33, matrix products, attend_dense(): jnp.einsum('hqk,kd->hqd', weights, kv_pair[1], preferred_element_type=jnp...  17.7 us
    all_gather x1, blocking collectives, body(): own_pair = lax.all_gather(own_slice, 'head', axis=1, tiled=True)  13.5 us
    dot_general x33, matrix products, attend_dense(): jnp.einsum('qhd,kd->hqk', query_heads, kv_pair[0], preferred_element_type...  12.7 us
    reduce_sum x33, other arithmetic, attend_dense(): totals = totals * factor + jnp.sum(exp_terms, axis=2)  10.5 us
  transfers between devices with their start and end apart: 32, of which 32 were waited for; matrix products, arithmetic and copies ran while one was open for 0% of the time, Pallas kernels for 0%

commit v1 on v0

v1 whole, which is shorter than its diff:
```python
import functools
import math

import jax
import jax.numpy as jnp
from jax import lax
from jax.experimental import pallas as pl
from jax.experimental.pallas import tpu as pltpu
from jax.sharding import PartitionSpec as P

HD = 128
PAGE = 128
NX, NY, NZ = 4, 4, 16
REQS = 16
SCALE = math.log2(math.e) / math.sqrt(HD)
LOW = -1e15
BIG = 1e30
NT = (((1,), (1,)), ((), ()))
NN = (((1,), (0,)), ((), ()))
MESH = pl.DeviceIdType.MESH
HALFWAY = NZ // 2


def dot(a, b, dims):
    return lax.dot_general(a, b, dims, preferred_element_type=jnp.float32)


def kernel(q_ref, k_ref, v_ref, len_ref, o_ref,
           qbuf, raw, kv, acc, mrow, starts, obuf, lbuf, osend, lsend,
           q_ss, q_rs, i_ss, i_rs, z_ss, z_rs, x_ss, x_rs, d_ss, d_rs, o_ss, o_rs, l_ss, l_rs):
    rows = q_ref.shape[0]
    seq = lax.axis_index("seq")
    head = lax.axis_index("head")
    x, z = seq // NZ, seq % NZ
    y, c = head // 2, head % 2
    way = 1 - 2 * c

    def at(dx, dy, dz, core):
        xx = (x + dx + NX) % NX
        yy = (y + dy) % NY
        zz = (z + dz + NZ) % NZ
        return (xx * NZ + zz, yy * 2 + core)

    barrier = pltpu.get_barrier_semaphore()
    partners = [at(0, 0, 0, 1 - c), at(0, 0, 1, c), at(0, 0, -1, c)]
    partners += [at(dx, 0, 0, core) for dx in (1, -1, 2) for core in (c, 1 - c)]
    partners += [at(0, dy, 0, c) for dy in (1, 2, 3)]
    for partner in partners:
        pl.semaphore_signal(barrier, inc=1, device_id=partner, device_id_type=MESH)

    raw[0, c, 0] = k_ref[...]
    raw[0, c, 1] = v_ref[...]
    qbuf[0] = q_ref[...]
    acc[...] = jnp.zeros_like(acc)
    mrow[...] = jnp.full_like(mrow, LOW)
    row_page = seq * (rows // PAGE) + lax.broadcasted_iota(jnp.int32, (1, rows), 1) // PAGE
    start = jnp.int32(0)
    found = jnp.zeros((1, rows), jnp.int32)
    for r in range(REQS):
        found = jnp.maximum(found, jnp.where(row_page >= start, start, 0))
        start = start + len_ref[r]
    starts[...] = found

    pl.semaphore_wait(barrier, len(partners))

    def remote(src, dst, ssem, rsem, to):
        return pltpu.make_async_remote_copy(
            src_ref=src, dst_ref=dst, send_sem=ssem, recv_sem=rsem, device_id=to, device_id_type=MESH)

    def init_copy(n):
        dx, core = ((0, 1 - c), (1, c), (1, 1 - c), (2, c), (2, 1 - c))[n]
        return remote(raw.at[0, c], raw.at[dx, c], i_ss.at[n], i_rs.at[n], at(dx, 0, 0, core))

    def init_wait(n):
        dx, core = ((0, 1 - c), (1, c), (1, 1 - c), (2, c), (2, 1 - c))[n]
        remote(raw.at[dx, core], raw.at[dx, core], i_ss.at[n], i_rs.at[n], at(0, 0, 0, 1 - c)).wait_recv()

    def q_copy(j):
        return remote(qbuf.at[0], qbuf.at[j], q_ss.at[j], q_rs.at[j], at(0, NY - j, 0, c))

    def zpos(t):
        return (z - way * t + 2 * NZ) % NZ

    def zother(t):
        return (z + way * t + 2 * NZ) % NZ

    def slot(dx, zz):
        return dx * NZ + zz

    def far(zz):
        return jnp.where(zz < z, 0, 2)

    def z_copy(part, t):
        s = slot(2 * part, zpos(t - 1))
        return remote(kv.at[s], kv.at[s], z_ss.at[part, t], z_rs.at[part, t], at(0, 0, way, c))

    def z_wait(part, t):
        s = slot(2 * part, zpos(t))
        remote(kv.at[s], kv.at[s], z_ss.at[part, t], z_rs.at[part, t], at(0, 0, way, c)).wait_recv()

    def x_copy(t):
        zz = zpos(t)
        return remote(kv.at[slot(0, zz)], kv.at[slot(1, zz)], x_ss.at[t], x_rs.at[t], at(1, 0, 0, c))

    def x_wait(t):
        s = slot(1, zpos(t))
        remote(kv.at[s], kv.at[s], x_ss.at[t], x_rs.at[t], at(1, 0, 0, c)).wait_recv()

    def d_slot(part, zz):
        return slot(1, zz) if part else slot(far(zz), zz)

    def d_copy(part, t):
        s = d_slot(part, zpos(t))
        return remote(kv.at[s], kv.at[s], d_ss.at[part, t], d_rs.at[part, t], at(0, 0, 0, 1 - c))

    def d_wait(part, t):
        s = d_slot(part, zother(t))
        remote(kv.at[s], kv.at[s], d_ss.at[part, t], d_rs.at[part, t], at(0, 0, 0, 1 - c)).wait_recv()

    def assemble(dx):
        s = slot(dx, z)
        kv[s, 0] = jnp.concatenate([raw[dx, 0, 0], raw[dx, 1, 0]], axis=0)
        values = jnp.concatenate([raw[dx, 0, 1], raw[dx, 1, 1]], axis=0)
        kv[s, 1] = values.T

    def ring(t):
        z_wait(0, t)

        @pl.when((t < HALFWAY - 1) | ((t < HALFWAY) & (c == 0)))
        def _():
            z_copy(0, t + 1).start()
        x_copy(t).start()
        z_wait(1, t)

        @pl.when((t < HALFWAY - 1) | ((t < HALFWAY) & (c == 0)))
        def _():
            z_copy(1, t + 1).start()
        d_copy(0, t).start()

    def across(t):
        x_wait(t)
        d_copy(1, t).start()

    def page_of(dx, zz):
        return ((x - dx) * NZ + zz) * (rows // PAGE) + y

    def chunk(pages, heads, diagonal=None, after=None):
        slots = [slot(dx, zz) for dx, zz in pages]
        ks = jnp.concatenate([kv[s, 0] for s in slots], axis=0)
        vt = jnp.concatenate([kv[s, 1] for s in slots], axis=1)
        vt = jnp.concatenate([vt, jnp.ones((16, vt.shape[1]), jnp.bfloat16)], axis=0)
        first = starts[...]
        bias = [jnp.where(first <= page_of(dx, zz), 0.0, -BIG) for dx, zz in pages]
        if diagonal is not None:
            key = y * PAGE + lax.broadcasted_iota(jnp.int32, (PAGE, rows), 0)
            row = lax.broadcasted_iota(jnp.int32, (PAGE, rows), 1)
            causal = key <= row
        scores = [dot(ks, qbuf[h], NT) for h in heads]
        for h, st in zip(heads, scores):
            old = mrow[h]
            new = old
            parts = []
            for n in range(len(pages)):
                part = st[n * PAGE:(n + 1) * PAGE] * SCALE
                if n == diagonal:
                    part = jnp.where(causal, part, -BIG)
                parts.append(part)
                new = jnp.maximum(new, jnp.max(part, axis=0, keepdims=True) + bias[n])
            terms = [jnp.exp2(parts[n] - (new - bias[n])) for n in range(len(pages))]
            factor = jnp.exp2(old - new)
            mrow[h] = new
            update = dot(vt, jnp.concatenate(terms, axis=0).astype(jnp.bfloat16), NN)
            acc[h] = acc[h] * factor + update
            if after is not None:
                after(h)

    def finish(h):
        total = jnp.maximum(acc[h, HD:HD + 1, :], 1e-30)
        part = acc[h, :HD, :] / total
        level = mrow[h] + jnp.log2(total)
        return part, level

    def o_copy(j):
        return remote(osend.at[j - 1], obuf.at[j - 1], o_ss.at[j], o_rs.at[j], at(0, j, 0, c))

    def l_copy(j):
        return remote(lsend.at[j - 1], lbuf.at[j - 1], l_ss.at[j], l_rs.at[j], at(0, j, 0, c))

    def give(h):
        if h > 0:
            part, level = finish(h)
            osend[h - 1] = part.astype(jnp.bfloat16)
            lsend[h - 1] = jnp.broadcast_to(level, lsend.shape[1:])
            o_copy(h).start()
            l_copy(h).start()

    for n in range(5):
        init_copy(n).start()
    for j in (1, 3, 2):
        q_copy(j).start()

    init_wait(0)
    assemble(0)
    z_copy(0, 1).start()
    init_wait(3)
    init_wait(4)
    assemble(2)
    z_copy(1, 1).start()
    init_wait(1)
    init_wait(2)
    assemble(1)
    own = [(0, z), (1, z), (2, z)]
    chunk(own, [0], 0)
    ring(1)
    for j in (1, 3):
        q_copy(j).wait_recv()
    chunk(own, [1, 3], 0)
    ring(2)
    across(1)
    q_copy(2).wait_recv()
    chunk(own, [2], 0)
    d_wait(0, 1)
    everyone = [2, 1, 3, 0]
    chunk([(far(zpos(1)), zpos(1)), (far(zother(1)), zother(1))], everyone)

    def turn(t, _):
        @pl.when((t < HALFWAY) | (c == 0))
        def _():
            ring(t)
        across(t - 1)
        d_wait(0, t - 1)
        d_wait(1, t - 2)
        chunk([(far(zpos(t - 1)), zpos(t - 1)), (far(zother(t - 1)), zother(t - 1)),
               (1, zpos(t - 2)), (1, zother(t - 2))], everyone)
        return 0

    lax.fori_loop(3, HALFWAY + 1, turn, 0)

    @pl.when(c == 0)
    def _():
        across(HALFWAY)

    @pl.when(c == 1)
    def _():
        d_wait(0, HALFWAY)
        d_wait(1, HALFWAY)
    d_wait(1, HALFWAY - 1)
    opposite = zpos(HALFWAY)
    chunk([(far(opposite), opposite), (1, zpos(HALFWAY - 1)), (1, zother(HALFWAY - 1)), (1, opposite)],
          everyone, after=give)

    part, level = finish(0)
    for j in (1, 2, 3):
        o_copy(j).wait_recv()
        l_copy(j).wait_recv()
    levels = [level] + [lbuf[j, 0:1, :] for j in range(3)]
    top = functools.reduce(jnp.maximum, levels)
    shares = [jnp.exp2(level - top) for level in levels]
    total = functools.reduce(jnp.add, shares)
    mixed = part * (shares[0] / total)
    for j in range(3):
        mixed = mixed + obuf[j].astype(jnp.float32) * (shares[j + 1] / total)
    o_ref[...] = mixed.T.astype(o_ref.dtype)

    for n in range(5):
        init_copy(n).wait_send()
    for j in (1, 2, 3):
        q_copy(j).wait_send()
        o_copy(j).wait_send()
        l_copy(j).wait_send()

    def drain(t, _):
        for part in (0, 1):
            z_copy(part, t).wait_send()
            d_copy(part, t).wait_send()
        x_copy(t).wait_send()
        return 0

    lax.fori_loop(1, HALFWAY, drain, 0)

    @pl.when(c == 0)
    def _():
        drain(HALFWAY, 0)


def body(queries, keys, values, req_lengths):
    rows = queries.shape[0]
    bf, f32, dma = jnp.bfloat16, jnp.float32, pltpu.SemaphoreType.DMA
    n = HALFWAY + 1
    return pl.pallas_call(
        kernel,
        out_shape=jax.ShapeDtypeStruct((rows, HD), bf),
        in_specs=[pl.BlockSpec(memory_space=pltpu.VMEM)] * 3 + [pl.BlockSpec(memory_space=pltpu.SMEM)],
        out_specs=pl.BlockSpec(memory_space=pltpu.VMEM),
        scratch_shapes=[
            pltpu.VMEM((NY, rows, HD), bf),
            pltpu.VMEM((3, 2, 2, PAGE // 2, HD), bf),
            pltpu.VMEM((3 * NZ, 2, PAGE, HD), bf),
            pltpu.VMEM((NY, HD + 16, rows), f32),
            pltpu.VMEM((NY, 1, rows), f32),
            pltpu.VMEM((1, rows), jnp.int32),
            pltpu.VMEM((NY - 1, HD, rows), bf),
            pltpu.VMEM((NY - 1, 8, rows), f32),
            pltpu.VMEM((NY - 1, HD, rows), bf),
            pltpu.VMEM((NY - 1, 8, rows), f32),
            dma((NY,)), dma((NY,)),
            dma((5,)), dma((5,)),
            dma((2, n)), dma((2, n)),
            dma((n,)), dma((n,)),
            dma((2, n)), dma((2, n)),
            dma((NY,)), dma((NY,)),
            dma((NY,)), dma((NY,)),
        ],
        compiler_params=pltpu.CompilerParams(
            collective_id=0, has_side_effects=True, vmem_limit_bytes=48 * 2**20),
    )(queries, keys, values, req_lengths)


def solution(mesh):
    placed = (P("seq", "head"), P(("seq", "head"), None), P(("seq", "head"), None), P())
    return jax.shard_map(
        body, mesh=mesh, in_specs=placed, out_specs=P("seq", "head"), check_vma=False
    )
```

time: 420 us -> 64.6 us (0.15)
  the two profiles are of different devices: /device:TPU:6 before, /device:TPU:1 now
where the time goes in v1:
time: 64.6 us; the launch traced here: 64.3 us
  Pallas kernels  60.6 us (94%)
  local copies, waits for them, and re-layouts  3.65 us (6%)
    pallas_call x1, Pallas kernels, body(): pl.pallas_call(kernel, out_shape=jax.ShapeDtypeStruct((rows, HD), bf), in...  60.6 us
    unnamed x9, local copies, waits for them, and re-layouts  3.65 us

profile of v1, /device:TPU:1, one launch (start us, length us, event | category | flops | bytes accessed | tf_op | source)
XLA Modules:
  0.0 64.3 jit_solution(8509059882188077544)
XLA Ops:
  0.0 0.0 copy-start
  0.0 0.9 %copy-done = bf16[512,128]{1,0:T(8,128)(2,1)S(1)} copy-done((bf16[512,128]{1,0:T(8,128)(2,1)S(1)}, bf16[512,128]{1,0:T(8,128)(2,1)}, u32[]{:S(2)}) %copy-start) | copy-done | bytes 131096
  0.9 0.0 copy-start.1
  0.9 0.7 %copy-done.1 = bf16[64,128]{1,0:T(8,128)(2,1)S(1)} copy-done((bf16[64,128]{1,0:T(8,128)(2,1)S(1)}, bf16[64,128]{1,0:T(8,128)(2,1)}, u32[]{:S(2)}) %copy-start.1) | copy-done | bytes 16408
  1.6 0.0 copy-start.2
  1.6 0.7 %copy-done.2 = bf16[64,128]{1,0:T(8,128)(2,1)S(1)} copy-done((bf16[64,128]{1,0:T(8,128)(2,1)S(1)}, bf16[64,128]{1,0:T(8,128)(2,1)}, u32[]{:S(2)}) %copy-start.2) | copy-done | bytes 16408
  2.3 0.0 copy-start.3
  2.3 0.7 %copy-done.3 = s32[16]{0:T(128)S(1)} copy-done((s32[16]{0:T(128)S(1)}, s32[16]{0:T(128)}, u32[]{:S(2)}) %copy-start.3) | copy-done | bytes 88
  3.0 60.6 %shard_map.46 = bf16[512,128]{1,0:T(8,128)(2,1)S(1)} custom-call(bf16[512,128]{1,0:T(8,128)(2,1)S(1)} %copy-done, bf16[64,128]{1,0:T(8,128)(2,1)S(1)} %copy-done.1, bf16[64,128]{1,0:T(8,128)(2,1)S(1)} %copy-done.2, s32[16]{0:T(128)S(1)} %copy-done.3), custom_call_target="tpu_custom_call" | custom-call | tf_op jit(solution)/shard_map/pallas_call | solution.py:290
  63.6 0.7 %copy.6 = bf16[512,128]{1,0:T(8,128)(2,1)} copy(bf16[512,128]{1,0:T(8,128)(2,1)S(1)} %shard_map.46) | data formatting | bytes 262144
Async XLA Ops:
  0.0 0.9 %copy-start = (bf16[512,128]{1,0:T(8,128)(2,1)S(1)}, bf16[512,128]{1,0:T(8,128)(2,1)}, u32[]{:S(2)}) copy-start(bf16[512,128]{1,0:T(8,128)(2,1)} %q_ref.1) | copy-start | bytes 393220
  0.9 0.7 %copy-start.1 = (bf16[64,128]{1,0:T(8,128)(2,1)S(1)}, bf16[64,128]{1,0:T(8,128)(2,1)}, u32[]{:S(2)}) copy-start(bf16[64,128]{1,0:T(8,128)(2,1)} %k_ref.1) | copy-start | bytes 49156
  1.6 0.7 %copy-start.2 = (bf16[64,128]{1,0:T(8,128)(2,1)S(1)}, bf16[64,128]{1,0:T(8,128)(2,1)}, u32[]{:S(2)}) copy-start(bf16[64,128]{1,0:T(8,128)(2,1)} %v_ref.1) | copy-start | bytes 49156
  2.3 0.7 %copy-start.3 = (s32[16]{0:T(128)S(1)}, s32[16]{0:T(128)}, u32[]{:S(2)}) copy-start(s32[16]{0:T(128)} %len_ref.1) | copy-start | bytes 196

commit v2 on v1

v2 whole, which is shorter than its diff:
```python
import functools
import math

import jax
import jax.numpy as jnp
from jax import lax
from jax.experimental import pallas as pl
from jax.experimental.pallas import tpu as pltpu
from jax.sharding import PartitionSpec as P

HD = 128
PAGE = 128
NX, NY, NZ = 4, 4, 16
REQS = 16
SCALE = math.log2(math.e) / math.sqrt(HD)
LOW = -1e15
BIG = 1e30
NT = (((1,), (1,)), ((), ()))
NN = (((1,), (0,)), ((), ()))
MESH = pl.DeviceIdType.MESH


def dot(a, b, dims):
    return lax.dot_general(a, b, dims, preferred_element_type=jnp.float32)


def kernel(q_ref, k_ref, v_ref, len_ref, o_ref,
           qbuf, kv, acc, mrow, starts, obuf, lbuf, osend, lsend,
           in_sem, q_ss, q_rs, own_ss, own_rs, far_ss, near_ss, z_rs, x_ss, x_rs, d_ss, d_rs,
           o_ss, o_rs, l_ss, l_rs):
    rows = qbuf.shape[1]
    seq = lax.axis_index("seq")
    head = lax.axis_index("head")
    x, z = seq // NZ, seq % NZ
    y, c = head // 2, head % 2

    def at(dx, dy, dz, core):
        xx = (x + dx + NX) % NX
        yy = (y + dy) % NY
        zz = (z + dz + NZ) % NZ
        return (xx * NZ + zz, yy * 2 + core)

    def flip(u, v):
        return (u % 2 + v % 2) % 2 + 2 * ((u // 2 + v // 2) % 2)

    def plane(a, j):
        return 4 * flip(z // 4, a) + flip(z % 4, j)

    def along(a, j):
        return (x * NZ + plane(a, j), y * 2 + c)

    late = z >= NZ // 2
    sibling = at(0, 0, 0, 1 - c)
    barrier = pltpu.get_barrier_semaphore()
    partners = [sibling] + [along(1, 0), along(0, 1), along(0, 2), along(0, 3)]
    partners += [at(dx, 0, 0, c) for dx in (1, -1, 2)]
    partners += [at(0, dy, 0, c) for dy in (1, 2, 3)]
    for partner in partners:
        pl.semaphore_signal(barrier, inc=1, device_id=partner, device_id_type=MESH)

    @pl.when(jnp.logical_not(late))
    def _():
        for a in (2, 3):
            pl.semaphore_signal(barrier, inc=1, device_id=along(a, 0), device_id_type=MESH)

    def slot(dx, zz):
        return dx * NZ + zz

    inputs = [
        pltpu.make_async_copy(k_ref, kv.at[slot(0, z), c, 0], in_sem.at[0]),
        pltpu.make_async_copy(v_ref, kv.at[slot(0, z), c, 1], in_sem.at[1]),
        pltpu.make_async_copy(q_ref, qbuf.at[0], in_sem.at[2]),
    ]
    for copy in inputs:
        copy.start()

    acc[...] = jnp.zeros_like(acc)
    mrow[...] = jnp.full_like(mrow, LOW)
    row_page = seq * (rows // PAGE) + lax.broadcasted_iota(jnp.int32, (1, rows), 1) // PAGE
    start = jnp.int32(0)
    found = jnp.zeros((1, rows), jnp.int32)
    for r in range(REQS):
        found = jnp.maximum(found, jnp.where(row_page >= start, start, 0))
        start = start + len_ref[r]
    starts[...] = found

    @pl.when(x < 2)
    def _():
        kv[2 * NZ:] = jnp.zeros((NZ,) + kv.shape[1:], kv.dtype)

    for copy in inputs:
        copy.wait()
    pl.semaphore_wait(barrier, len(partners) + 2 * (z // (NZ // 2)))

    def remote(src, dst, ssem, rsem, to):
        return pltpu.make_async_remote_copy(
            src_ref=src, dst_ref=dst, send_sem=ssem, recv_sem=rsem, device_id=to, device_id_type=MESH)

    def q_copy(j):
        return remote(qbuf.at[0], qbuf.at[j], q_ss.at[j], q_rs.at[j], at(0, NY - j, 0, c))

    def half(dx, zz, core):
        return kv.at[slot(dx, zz), core]

    def own_copy():
        return remote(half(0, z, c), half(0, z, c), own_ss.at[0], own_rs.at[0], sibling)

    def far_copy(a):
        return remote(half(0, z, c), half(0, z, c), far_ss.at[a - 1], z_rs.at[z], along(a, 0))

    def near_copy(j, zz):
        return remote(half(0, zz, c), half(0, zz, c), near_ss.at[j - 1, zz // 4], z_rs.at[zz], along(0, j))

    def z_wait(zz):
        remote(half(0, zz, c), half(0, zz, c), far_ss.at[0], z_rs.at[zz], sibling).wait_recv()

    def x_copy(dx, zz):
        return remote(half(0, zz, c), half(dx, zz, c), x_ss.at[dx - 1, zz], x_rs.at[dx - 1, zz], at(dx, 0, 0, c))

    def x_wait(dx, zz):
        remote(half(dx, zz, c), half(dx, zz, c), x_ss.at[dx - 1, zz], x_rs.at[dx - 1, zz], sibling).wait_recv()

    def far(zz):
        return jnp.where(zz < z, 0, 2)

    def d_copy(part, zz, core):
        dx = 1 if part else far(zz)
        return remote(half(dx, zz, core), half(dx, zz, core), d_ss.at[part, zz], d_rs.at[part, zz], sibling)

    def pair(n):
        a, j = 2 * (n // 4), n % 4
        return plane(a, j), plane(a + 1, j)

    def share(zz):
        x_copy(1, zz).start()

        @pl.when((zz >= z) & (x < 2))
        def _():
            x_copy(2, zz).start()

        @pl.when(zz < z)
        def _():
            d_copy(0, zz, c).start()

    def spread(zz):
        for j in (1, 2, 3):
            near_copy(j, zz).start()

    def own_row(n):
        for zz in pair(n):
            z_wait(zz)
            share(zz)

    def other_half():
        for a in (2, 3):
            zz = plane(a, 0)
            z_wait(zz)
            spread(zz)

            @pl.when(jnp.logical_not(late))
            def _():
                far_copy(a).start()
            share(zz)

    def other_rows(n):
        for zz in pair(n):
            x_wait(1, zz)
            d_copy(1, zz, c).start()

            @pl.when((zz >= z) & (x >= 2))
            def _():
                x_wait(2, zz)
                d_copy(0, zz, c).start()

    def arrived(n):
        for zz in pair(n):
            d_copy(1, zz, 1 - c).wait_recv()

            @pl.when((zz < z) | (x >= 2))
            def _():
                d_copy(0, zz, 1 - c).wait_recv()

    def page_of(dx, zz):
        return ((x - dx) * NZ + zz) * (rows // PAGE) + y

    def chunk(pages, heads, diagonal=None, after=None):
        slots = [slot(dx, zz) for dx, zz in pages]
        ks = jnp.concatenate([kv[s, i, 0] for s in slots for i in (0, 1)], axis=0)
        vs = jnp.concatenate([kv[s, i, 1] for s in slots for i in (0, 1)], axis=0)
        vt = jnp.concatenate([vs.T, jnp.ones((16, vs.shape[0]), jnp.bfloat16)], axis=0)
        first = starts[...]
        bias = [jnp.where(first <= page_of(dx, zz), 0.0, -BIG) for dx, zz in pages]
        if diagonal is not None:
            key = y * PAGE + lax.broadcasted_iota(jnp.int32, (PAGE, rows), 0)
            row = lax.broadcasted_iota(jnp.int32, (PAGE, rows), 1)
            causal = key <= row
        scores = [dot(ks, qbuf[h], NT) for h in heads]
        for h, st in zip(heads, scores):
            old = mrow[h]
            new = old
            parts = []
            for n in range(len(pages)):
                part = st[n * PAGE:(n + 1) * PAGE] * SCALE
                if n == diagonal:
                    part = jnp.where(causal, part, -BIG)
                parts.append(part)
                new = jnp.maximum(new, jnp.max(part, axis=0, keepdims=True) + bias[n])
            terms = [jnp.exp2(parts[n] - (new - bias[n])) for n in range(len(pages))]
            factor = jnp.exp2(old - new)
            mrow[h] = new
            update = dot(vt, jnp.concatenate(terms, axis=0).astype(jnp.bfloat16), NN)
            acc[h] = acc[h] * factor + update
            if after is not None:
                after(h)

    def pages(n):
        a, b = pair(n)
        return [(far(a), a), (far(b), b), (1, a), (1, b)]

    def finish(h):
        total = jnp.maximum(acc[h, HD:HD + 1, :], 1e-30)
        part = acc[h, :HD, :] / total
        level = mrow[h] + jnp.log2(total)
        return part, level

    def o_copy(j):
        return remote(osend.at[j - 1], obuf.at[j - 1], o_ss.at[j], o_rs.at[j], at(0, j, 0, c))

    def l_copy(j):
        return remote(lsend.at[j - 1], lbuf.at[j - 1], l_ss.at[j], l_rs.at[j], at(0, j, 0, c))

    def give(h):
        if h > 0:
            part, level = finish(h)
            osend[h - 1] = part.astype(jnp.bfloat16)
            lsend[h - 1] = jnp.broadcast_to(level, lsend.shape[1:])
            o_copy(h).start()
            l_copy(h).start()

    @pl.when(late)
    def _():
        far_copy(2).start()
        far_copy(3).start()
    far_copy(1).start()
    own_copy().start()
    spread(z)
    share(z)
    for j in (1, 3, 2):
        q_copy(j).start()
    fourth = plane(1, 0)
    z_wait(fourth)
    spread(fourth)
    share(fourth)
    own_row(1)
    remote(half(0, z, 1 - c), half(0, z, 1 - c), own_ss.at[0], own_rs.at[0], sibling).wait_recv()
    for j in (1, 3, 2):
        q_copy(j).wait_recv()
    everyone = [2, 1, 3, 0]
    chunk([(0, z)], everyone, 0)

    def turn(n, _):
        @pl.when((n < 8) & (n != 4))
        def _():
            own_row(n)

        @pl.when(n == 4)
        def _():
            other_half()

        @pl.when((n >= 3) & (n < 8 + 3))
        def _():
            other_rows(n - 3)

        @pl.when(n >= 4)
        def _():
            arrived(n - 4)
            chunk(pages(n - 4), everyone)
        return 0

    lax.fori_loop(2, 7 + 4, turn, 0)
    arrived(7)
    chunk(pages(7), everyone, after=give)

    part, level = finish(0)
    for j in (1, 2, 3):
        o_copy(j).wait_recv()
        l_copy(j).wait_recv()
    levels = [level] + [lbuf[j, 0:1, :] for j in range(3)]
    top = functools.reduce(jnp.maximum, levels)
    shares = [jnp.exp2(level - top) for level in levels]
    total = functools.reduce(jnp.add, shares)
    mixed = part * (shares[0] / total)
    for j in range(3):
        mixed = mixed + obuf[j].astype(jnp.float32) * (shares[j + 1] / total)
    o_ref[...] = mixed.T.astype(o_ref.dtype)

    own_copy().wait_send()
    for a in (1, 2, 3):
        far_copy(a).wait_send()
    for j in (1, 2, 3):
        q_copy(j).wait_send()
        o_copy(j).wait_send()
        l_copy(j).wait_send()

    def drain_near(a, _):
        for j in (1, 2, 3):
            near_copy(j, a * 4 + z % 4).wait_send()
        return 0

    def drain(zz, _):
        x_copy(1, zz).wait_send()
        d_copy(1, zz, c).wait_send()

        @pl.when((zz >= z) & (x < 2))
        def _():
            x_copy(2, zz).wait_send()

        @pl.when((zz < z) | (x >= 2))
        def _():
            d_copy(0, zz, c).wait_send()
        return 0

    lax.fori_loop(0, 4, drain_near, 0)
    lax.fori_loop(0, NZ, drain, 0)


def body(queries, keys, values, req_lengths):
    rows = queries.shape[0]
    bf, f32, dma = jnp.bfloat16, jnp.float32, pltpu.SemaphoreType.DMA
    return pl.pallas_call(
        kernel,
        out_shape=jax.ShapeDtypeStruct((rows, HD), bf),
        in_specs=[pl.BlockSpec(memory_space=pl.ANY)] * 3 + [pl.BlockSpec(memory_space=pltpu.SMEM)],
        out_specs=pl.BlockSpec(memory_space=pltpu.VMEM),
        scratch_shapes=[
            pltpu.VMEM((NY, rows, HD), bf),
            pltpu.VMEM((3 * NZ, 2, 2, PAGE // 2, HD), bf),
            pltpu.VMEM((NY, HD + 16, rows), f32),
            pltpu.VMEM((NY, 1, rows), f32),
            pltpu.VMEM((1, rows), jnp.int32),
            pltpu.VMEM((NY - 1, HD, rows), bf),
            pltpu.VMEM((NY - 1, 8, rows), f32),
            pltpu.VMEM((NY - 1, HD, rows), bf),
            pltpu.VMEM((NY - 1, 8, rows), f32),
            dma((3,)),
            dma((NY,)), dma((NY,)),
            dma((1,)), dma((1,)),
            dma((3,)), dma((3, 4)), dma((NZ,)),
            dma((2, NZ)), dma((2, NZ)),
            dma((2, NZ)), dma((2, NZ)),
            dma((NY,)), dma((NY,)),
            dma((NY,)), dma((NY,)),
        ],
        compiler_params=pltpu.CompilerParams(
            collective_id=0, has_side_effects=True, vmem_limit_bytes=60 * 2**20),
    )(queries, keys, values, req_lengths)


def solution(mesh):
    placed = (P("seq", "head"), P(("seq", "head"), None), P(("seq", "head"), None), P())
    return jax.shard_map(
        body, mesh=mesh, in_specs=placed, out_specs=P("seq", "head"), check_vma=False
    )
```

time: 64.6 us -> 56.6 us (0.88)
  Pallas kernels: 60.6 us -> 54.9 us
  local copies, waits for them, and re-layouts: 3.65 us -> 1.57 us
    pallas_call x1, Pallas kernels: 60.6 us -> 54.9 us  [body(): pl.pallas_call(kernel, out_shape=jax.ShapeDtypeStruct((rows, HD), bf), in...]
    unnamed x9 -> x1, local copies, waits for them, and re-layouts: 3.65 us -> 1.57 us
where the time goes in v2:
time: 56.6 us; the launch traced here: 56.4 us
  Pallas kernels  54.9 us (97%)
  local copies, waits for them, and re-layouts  1.57 us (3%)
    pallas_call x1, Pallas kernels, body(): pl.pallas_call(kernel, out_shape=jax.ShapeDtypeStruct((rows, HD), bf), in...  54.9 us
    unnamed x1, local copies, waits for them, and re-layouts  1.57 us

profile of v2, /device:TPU:1, one launch (start us, length us, event | category | flops | bytes accessed | tf_op | source)
XLA Modules:
  0.0 56.4 jit_solution(6199104978071187911)
XLA Ops:
  0.0 54.9 %shard_map.46 = bf16[512,128]{1,0:T(8,128)(2,1)} custom-call(bf16[512,128]{1,0:T(8,128)(2,1)} %q_ref.1, bf16[64,128]{1,0:T(8,128)(2,1)} %k_ref.1, bf16[64,128]{1,0:T(8,128)(2,1)} %v_ref.1, s32[16]{0:T(128)} %len_ref.1), custom_call_target="tpu_custom_call" | custom-call | tf_op jit(solution)/shard_map/pallas_call | solution.py:330
  54.9 1.6 %copy.6 = bf16[512,128]{1,0:T(8,128)(2,1)} copy(bf16[512,128]{1,0:T(8,128)(2,1)} %shard_map.46) | data formatting | bytes 262144

commit v3 on v2

--- a/solution.py
+++ b/solution.py
@@ -26,7 +26,7 @@
 
 def kernel(q_ref, k_ref, v_ref, len_ref, o_ref,
            qbuf, kv, acc, mrow, starts, obuf, lbuf, osend, lsend,
-           in_sem, q_ss, q_rs, own_ss, own_rs, far_ss, near_ss, z_rs, x_ss, x_rs, d_ss, d_rs,
+           in_sem, hello, q_ss, q_rs, own_ss, own_rs, far_ss, near_ss, z_rs, x_ss, x_rs, d_ss, d_rs,
            o_ss, o_rs, l_ss, l_rs):
     rows = qbuf.shape[1]
     seq = lax.axis_index("seq")
@@ -84,6 +84,10 @@
         start = start + len_ref[r]
     starts[...] = found
 
+    @pl.when(x == 0)
+    def _():
+        kv[NZ:2 * NZ] = jnp.zeros((NZ,) + kv.shape[1:], kv.dtype)
+
     @pl.when(x < 2)
     def _():
         kv[2 * NZ:] = jnp.zeros((NZ,) + kv.shape[1:], kv.dtype)
@@ -132,7 +136,9 @@
         return plane(a, j), plane(a + 1, j)
 
     def share(zz):
-        x_copy(1, zz).start()
+        @pl.when(x < NX - 1)
+        def _():
+            x_copy(1, zz).start()
 
         @pl.when((zz >= z) & (x < 2))
         def _():
@@ -152,20 +158,24 @@
             share(zz)
 
     def other_half():
+        @pl.when(jnp.logical_not(late))
+        def _():
+            for a in (2, 3):
+                pl.semaphore_wait(hello.at[a - 2], 1)
+                far_copy(a).start()
+
         for a in (2, 3):
             zz = plane(a, 0)
             z_wait(zz)
             spread(zz)
-
-            @pl.when(jnp.logical_not(late))
-            def _():
-                far_copy(a).start()
             share(zz)
 
     def other_rows(n):
         for zz in pair(n):
-            x_wait(1, zz)
-            d_copy(1, zz, c).start()
+            @pl.when(x > 0)
+            def _():
+                x_wait(1, zz)
+                d_copy(1, zz, c).start()
 
             @pl.when((zz >= z) & (x >= 2))
             def _():
@@ -174,7 +184,9 @@
 
     def arrived(n):
         for zz in pair(n):
-            d_copy(1, zz, 1 - c).wait_recv()
+            @pl.when(x > 0)
+            def _():
+                d_copy(1, zz, 1 - c).wait_recv()
 
             @pl.when((zz < z) | (x >= 2))
             def _():
@@ -219,7 +231,7 @@
 
     def finish(h):
         total = jnp.maximum(acc[h, HD:HD + 1, :], 1e-30)
-        part = acc[h, :HD, :] / total
+        part = acc[h, :HD, :] * (1.0 / total)
         level = mrow[h] + jnp.log2(total)
         return part, level
 
@@ -239,6 +251,8 @@
 
     @pl.when(late)
     def _():
+        for a in (2, 3):
+            pl.semaphore_signal(hello.at[a - 2], inc=1, device_id=along(a, 0), device_id_type=MESH)
         far_copy(2).start()
         far_copy(3).start()
     far_copy(1).start()
@@ -252,11 +266,13 @@
     spread(fourth)
     share(fourth)
     own_row(1)
-    remote(half(0, z, 1 - c), half(0, z, 1 - c), own_ss.at[0], own_rs.at[0], sibling).wait_recv()
-    for j in (1, 3, 2):
-        q_copy(j).wait_recv()
-    everyone = [2, 1, 3, 0]
-    chunk([(0, z)], everyone, 0)
+    given = [2, 1, 3]
+
+    def begin():
+        remote(half(0, z, 1 - c), half(0, z, 1 - c), own_ss.at[0], own_rs.at[0], sibling).wait_recv()
+        for j in (1, 3, 2):
+            q_copy(j).wait_recv()
+        chunk([(0, z)], given, 0)
 
     def turn(n, _):
         @pl.when((n < 8) & (n != 4))
@@ -271,16 +287,26 @@
         def _():
             other_rows(n - 3)
 
+        @pl.when(n == 4)
+        def _():
+            begin()
+
         @pl.when(n >= 4)
         def _():
             arrived(n - 4)
-            chunk(pages(n - 4), everyone)
+            chunk(pages(n - 4), given)
         return 0
 
     lax.fori_loop(2, 7 + 4, turn, 0)
     arrived(7)
-    chunk(pages(7), everyone, after=give)
-
+    chunk(pages(7), given, after=give)
+    chunk([(0, z)], [0], 0)
+
+    def own_head(n, _):
+        chunk(pages(n), [0])
+        return 0
+
+    lax.fori_loop(0, 8, own_head, 0)
     part, level = finish(0)
     for j in (1, 2, 3):
         o_copy(j).wait_recv()
@@ -308,8 +334,13 @@
         return 0
 
     def drain(zz, _):
-        x_copy(1, zz).wait_send()
-        d_copy(1, zz, c).wait_send()
+        @pl.when(x < NX - 1)
+        def _():
+            x_copy(1, zz).wait_send()
+
+        @pl.when(x > 0)
+        def _():
+            d_copy(1, zz, c).wait_send()
 
         @pl.when((zz >= z) & (x < 2))
         def _():
@@ -342,7 +373,7 @@
             pltpu.VMEM((NY - 1, 8, rows), f32),
             pltpu.VMEM((NY - 1, HD, rows), bf),
             pltpu.VMEM((NY - 1, 8, rows), f32),
-            dma((3,)),
+            dma((3,)), pltpu.SemaphoreType.REGULAR((6,)),
             dma((NY,)), dma((NY,)),
             dma((1,)), dma((1,)),
             dma((3,)), dma((3, 4)), dma((NZ,)),

time: 56.6 us -> 54.6 us (0.965)
  the two profiles are of different devices: /device:TPU:1 before, /device:TPU:6 now
where the time goes in v3:
time: 54.6 us; the launch traced here: 53.8 us
  Pallas kernels  52.3 us (96%)
  local copies, waits for them, and re-layouts  1.57 us (3%)
    pallas_call x1, Pallas kernels, body(): pl.pallas_call(kernel, out_shape=jax.ShapeDtypeStruct((rows, HD), bf), in...  52.3 us
    unnamed x1, local copies, waits for them, and re-layouts  1.57 us

profile of v3, /device:TPU:6, one launch (start us, length us, event | category | flops | bytes accessed | tf_op | source)
XLA Modules:
  0.0 53.8 jit_solution(1777016682540923971)
XLA Ops:
  0.0 52.3 %shard_map.46 = bf16[512,128]{1,0:T(8,128)(2,1)} custom-call(bf16[512,128]{1,0:T(8,128)(2,1)} %q_ref.1, bf16[64,128]{1,0:T(8,128)(2,1)} %k_ref.1, bf16[64,128]{1,0:T(8,128)(2,1)} %v_ref.1, s32[16]{0:T(128)} %len_ref.1), custom_call_target="tpu_custom_call" | custom-call | tf_op jit(solution)/shard_map/pallas_call | solution.py:361
  52.3 1.6 %copy.6 = bf16[512,128]{1,0:T(8,128)(2,1)} copy(bf16[512,128]{1,0:T(8,128)(2,1)} %shard_map.46) | data formatting | bytes 262144

commit v4 on v3

--- a/solution.py
+++ b/solution.py
@@ -73,24 +73,6 @@
     ]
     for copy in inputs:
         copy.start()
-
-    acc[...] = jnp.zeros_like(acc)
-    mrow[...] = jnp.full_like(mrow, LOW)
-    row_page = seq * (rows // PAGE) + lax.broadcasted_iota(jnp.int32, (1, rows), 1) // PAGE
-    start = jnp.int32(0)
-    found = jnp.zeros((1, rows), jnp.int32)
-    for r in range(REQS):
-        found = jnp.maximum(found, jnp.where(row_page >= start, start, 0))
-        start = start + len_ref[r]
-    starts[...] = found
-
-    @pl.when(x == 0)
-    def _():
-        kv[NZ:2 * NZ] = jnp.zeros((NZ,) + kv.shape[1:], kv.dtype)
-
-    @pl.when(x < 2)
-    def _():
-        kv[2 * NZ:] = jnp.zeros((NZ,) + kv.shape[1:], kv.dtype)
 
     for copy in inputs:
         copy.wait()
@@ -245,7 +227,7 @@
         if h > 0:
             part, level = finish(h)
             osend[h - 1] = part.astype(jnp.bfloat16)
-            lsend[h - 1] = jnp.broadcast_to(level, lsend.shape[1:])
+            lsend[h - 1] = level
             o_copy(h).start()
             l_copy(h).start()
 
@@ -261,6 +243,24 @@
     share(z)
     for j in (1, 3, 2):
         q_copy(j).start()
+    acc[...] = jnp.zeros_like(acc)
+    mrow[...] = jnp.full_like(mrow, LOW)
+    row_page = seq * (rows // PAGE) + lax.broadcasted_iota(jnp.int32, (1, rows), 1) // PAGE
+    start = jnp.int32(0)
+    found = jnp.zeros((1, rows), jnp.int32)
+    for r in range(REQS):
+        found = jnp.maximum(found, jnp.where(row_page >= start, start, 0))
+        start = start + len_ref[r]
+    starts[...] = found
+
+    @pl.when(x == 0)
+    def _():
+        kv[NZ:2 * NZ] = jnp.zeros((NZ,) + kv.shape[1:], kv.dtype)
+
+    @pl.when(x < 2)
+    def _():
+        kv[2 * NZ:] = jnp.zeros((NZ,) + kv.shape[1:], kv.dtype)
+
     fourth = plane(1, 0)
     z_wait(fourth)
     spread(fourth)
@@ -307,11 +307,43 @@
         return 0
 
     lax.fori_loop(0, 8, own_head, 0)
+    own_copy().wait_send()
+    for a in (1, 2, 3):
+        far_copy(a).wait_send()
+    for j in (1, 2, 3):
+        q_copy(j).wait_send()
+
+    def drain_near(a, _):
+        for j in (1, 2, 3):
+            near_copy(j, a * 4 + z % 4).wait_send()
+        return 0
+
+    def drain(zz, _):
+        @pl.when(x < NX - 1)
+        def _():
+            x_copy(1, zz).wait_send()
+
+        @pl.when(x > 0)
+        def _():
+            d_copy(1, zz, c).wait_send()
+
+        @pl.when((zz >= z) & (x < 2))
+        def _():
+            x_copy(2, zz).wait_send()
+
+        @pl.when((zz < z) | (x >= 2))
+        def _():
+            d_copy(0, zz, c).wait_send()
+        return 0
+
+    lax.fori_loop(0, 4, drain_near, 0)
+    lax.fori_loop(0, NZ, drain, 0)
+
     part, level = finish(0)
     for j in (1, 2, 3):
         o_copy(j).wait_recv()
         l_copy(j).wait_recv()
-    levels = [level] + [lbuf[j, 0:1, :] for j in range(3)]
+    levels = [level] + [lbuf[j] for j in range(3)]
     top = functools.reduce(jnp.maximum, levels)
     shares = [jnp.exp2(level - top) for level in levels]
     total = functools.reduce(jnp.add, shares)
@@ -320,39 +352,9 @@
         mixed = mixed + obuf[j].astype(jnp.float32) * (shares[j + 1] / total)
     o_ref[...] = mixed.T.astype(o_ref.dtype)
 
-    own_copy().wait_send()
-    for a in (1, 2, 3):
-        far_copy(a).wait_send()
     for j in (1, 2, 3):
-        q_copy(j).wait_send()
         o_copy(j).wait_send()
         l_copy(j).wait_send()
-
-    def drain_near(a, _):
-        for j in (1, 2, 3):
-            near_copy(j, a * 4 + z % 4).wait_send()
-        return 0
-
-    def drain(zz, _):
-        @pl.when(x < NX - 1)
-        def _():
-            x_copy(1, zz).wait_send()
-
-        @pl.when(x > 0)
-        def _():
-            d_copy(1, zz, c).wait_send()
-
-        @pl.when((zz >= z) & (x < 2))
-        def _():
-            x_copy(2, zz).wait_send()
-
-        @pl.when((zz < z) | (x >= 2))
-        def _():
-            d_copy(0, zz, c).wait_send()
-        return 0
-
-    lax.fori_loop(0, 4, drain_near, 0)
-    lax.fori_loop(0, NZ, drain, 0)
 
 
 def body(queries, keys, values, req_lengths):
@@ -370,9 +372,9 @@
             pltpu.VMEM((NY, 1, rows), f32),
             pltpu.VMEM((1, rows), jnp.int32),
             pltpu.VMEM((NY - 1, HD, rows), bf),
-            pltpu.VMEM((NY - 1, 8, rows), f32),
+            pltpu.VMEM((NY - 1, 1, rows), f32),
             pltpu.VMEM((NY - 1, HD, rows), bf),
-            pltpu.VMEM((NY - 1, 8, rows), f32),
+            pltpu.VMEM((NY - 1, 1, rows), f32),
             dma((3,)), pltpu.SemaphoreType.REGULAR((6,)),
             dma((NY,)), dma((NY,)),
             dma((1,)), dma((1,)),

time: 54.6 us -> 53.7 us (0.984)
  Pallas kernels: 52.3 us -> 51.4 us
    pallas_call x1, Pallas kernels: 52.3 us -> 51.4 us  [body(): pl.pallas_call(kernel, out_shape=jax.ShapeDtypeStruct((rows, HD), bf), in...]
where the time goes in v4:
time: 53.7 us; the launch traced here: 52.9 us
  Pallas kernels  51.4 us (96%)
  local copies, waits for them, and re-layouts  1.57 us (3%)
    pallas_call x1, Pallas kernels, body(): pl.pallas_call(kernel, out_shape=jax.ShapeDtypeStruct((rows, HD), bf), in...  51.4 us
    unnamed x1, local copies, waits for them, and re-layouts  1.57 us

profile of v4, /device:TPU:6, one launch (start us, length us, event | category | flops | bytes accessed | tf_op | source)
XLA Modules:
  0.0 52.9 jit_solution(14617279651985017408)
XLA Ops:
  0.0 51.4 %shard_map.46 = bf16[512,128]{1,0:T(8,128)(2,1)} custom-call(bf16[512,128]{1,0:T(8,128)(2,1)} %q_ref.1, bf16[64,128]{1,0:T(8,128)(2,1)} %k_ref.1, bf16[64,128]{1,0:T(8,128)(2,1)} %v_ref.1, s32[16]{0:T(128)} %len_ref.1), custom_call_target="tpu_custom_call" | custom-call | tf_op jit(solution)/shard_map/pallas_call | solution.py:363
  51.4 1.6 %copy.6 = bf16[512,128]{1,0:T(8,128)(2,1)} copy(bf16[512,128]{1,0:T(8,128)(2,1)} %shard_map.46) | data formatting | bytes 262144
